TPU v7x, 32 devices: a whole 2x2x4 slice. The times are simulated.
32 devices in a mesh: dp: 2 (over x), row: 4 (over y, core), col: 4 (over z).
Axes of the slice: x: 2, y: 2, z: 4, core: 2. Of those that a mesh axis runs over, the one named last changes fastest.
Arguments:
- inputs: float32 [4096, 1088], P(('dp', 'row')), may hold values from -6 to 6
- segment_ids: int32 [4096], P(('dp', 'row')), may hold values from 0 to 2, as said below
- head_map: int32 [17], replicated, may hold values from 0 to 31, as said below
- gain_one: float32 [2, 1088], replicated, may hold values from 0.5 to 1.5
- shift_one: float32 [2, 1088], replicated, may hold values from -1.2 to 1.2
- gain_two: float32 [2, 1088], replicated, may hold values from 0.5 to 1.5
- shift_two: float32 [2, 1088], replicated, may hold values from -1.2 to 1.2
- w_qkv: bfloat16 [2, 1088, 6144], P(None, 'row', 'col'), may hold values from -0.1875 to 0.1875
- w_out: bfloat16 [2, 2048, 1088], P(None, 'col', 'row'), may hold values from -1.5 to 1.5
- w_up: bfloat16 [2, 1088, 4352], P(None, 'row', 'col'), may hold values from -0.1875 to 0.1875
- w_down: bfloat16 [2, 4352, 1088], P(None, 'col', 'row'), may hold values from -0.09375 to 0.09375
- cotangent: float32 [4096, 1088], P(('dp', 'row')), may hold values from -6 to 6
Outputs:
- output: float32 [4096, 1088], P(('dp', 'row'))
- grad_inputs: float32 [4096, 1088], P(('dp', 'row'))
- grad_gain_one: float32 [2, 1088], replicated
- grad_shift_one: float32 [2, 1088], replicated
- grad_gain_two: float32 [2, 1088], replicated
- grad_shift_two: float32 [2, 1088], replicated
- grad_qkv: float32 [2, 1088, 6144], P(None, 'row', 'col')
- grad_out: float32 [2, 2048, 1088], P(None, 'col', 'row')
- grad_up: float32 [2, 1088, 4352], P(None, 'row', 'col')
- grad_down: float32 [2, 4352, 1088], P(None, 'col', 'row')
Inputs may be any that keep to these rules, and one draw needn't show every extreme that they name: `segment_ids`: within each sequence of 2048 tokens the ids are 0, 1, 2 in order, never falling; document 1 starts before token 512 and ends after token 1536 of its sequence. `head_map`: the heads use distinct slots; slot s lies on index s // 8 of col; each index of col holds at most 8 heads, and one holds exactly 8.
All inputs are finite; a program needn't handle non-finite values.
Results may differ from a plain program's by a relative error of at most 0.023.
Values may be sent and summed in bfloat16 or wider, within the bound.
A program may use at most 256 MiB of HBM per device.

v0:
```python
from functools import partial

import jax
import jax.numpy as jnp
from jax import lax
from jax.sharding import PartitionSpec as P

HD = 64
LAYERS = 2


norm_eps = 1e-05
masked_score = -1e30
start_score = -1e20


def norm_forward(stream, scales, shifts):
    centre = stream - jnp.mean(stream, axis=-1, keepdims=True)
    inverse = lax.rsqrt(jnp.mean(centre * centre, axis=-1, keepdims=True) + norm_eps)
    standard = centre * inverse
    return (standard * scales + shifts, standard, inverse)


def norm_backward(incoming, standard, inverse, scales):
    scaled = incoming * scales
    grad_stream = inverse * (
        scaled
        - jnp.mean(scaled, axis=-1, keepdims=True)
        - standard * jnp.mean(scaled * standard, axis=-1, keepdims=True)
    )
    return (grad_stream, jnp.sum(incoming * standard, axis=0), jnp.sum(incoming, axis=0))


def full_inputs(shard):
    return lax.all_gather(shard, "row", axis=0, tiled=True)


def full_outputs(shard):
    return lax.all_gather(shard, "row", axis=1, tiled=True)


def column_sum(pieces):
    return lax.psum(pieces.astype(jnp.bfloat16), "col").astype(jnp.float32)


def feature_sum(pieces):
    return lax.psum(pieces.astype(jnp.bfloat16), "col").astype(jnp.float32)


def contract_rows(left, right):
    return lax.dot_general(
        left, right, (((0,), (0,)), ((), ())), preferred_element_type=jnp.float32
    )


def contract_cols(left, right):
    return lax.dot_general(
        left, right, (((1,), (1,)), ((), ())), preferred_element_type=jnp.float32
    )


def weight_share(left, right):
    width = left.shape[1]
    tokens_here = left.shape[0]
    row_count = lax.axis_size("row")
    data_count = lax.axis_size("dp")
    piece_rows = width // (row_count * data_count)
    reordered = left.reshape(tokens_here, row_count, data_count, piece_rows)
    reordered = reordered.transpose(0, 2, 1, 3).reshape(tokens_here, width)
    return lax.psum_scatter(
        contract_rows(reordered, right).astype(jnp.bfloat16),
        ("dp", "row"),
        scatter_dimension=0,
        tiled=True,
    ).astype(jnp.float32)


def finish_layer(share_qkv, share_out, share_up, share_down):
    return (
        lax.all_gather(share_qkv.astype(jnp.bfloat16), "dp", axis=0, tiled=True).astype(
            share_qkv.dtype
        ),
        lax.all_gather(share_out.astype(jnp.bfloat16), "dp", axis=0, tiled=True).astype(
            share_out.dtype
        ),
        lax.all_gather(share_up.astype(jnp.bfloat16), "dp", axis=0, tiled=True).astype(
            share_up.dtype
        ),
        lax.all_gather(share_down.astype(jnp.bfloat16), "dp", axis=0, tiled=True).astype(
            share_down.dtype
        ),
    )


def visible(count, seg_all, query_pos, query_seg):
    key_pos = jnp.arange(count, dtype=jnp.int32)
    return (key_pos[None, :] <= query_pos[:, None]) & (seg_all[None, :] == query_seg[:, None])


def attend(queries, pairs, seg_all, query_pos, query_seg):
    head_dim = queries.shape[-1]
    slot_count = queries.shape[1]
    row_count = queries.shape[0]
    score_scale = head_dim ** (-0.5)

    def add_piece(state_now, block_kv, offset):
        running, denominator, weighted = state_now
        key_part = block_kv[..., :head_dim]
        value_part = block_kv[..., head_dim:]
        logits = (
            jnp.einsum("qsd,ksd->sqk", queries, key_part, preferred_element_type=jnp.float32)
            * score_scale
        )
        logits = jnp.where(
            visible(block_kv.shape[0], seg_all, query_pos, query_seg)[None], logits, masked_score
        )
        newest = jnp.maximum(running, jnp.max(logits, axis=-1))
        factor = jnp.exp(running - newest)
        weights = jnp.exp(logits - newest[..., None])
        denominator = jnp.sum(weights, axis=-1)
        weighted = weighted * factor.T[..., None] + jnp.einsum(
            "sqk,ksd->qsd",
            weights.astype(jnp.bfloat16),
            value_part,
            preferred_element_type=jnp.float32,
        )
        return (newest, denominator, weighted)

    initial = (
        jnp.full((slot_count, row_count), start_score, jnp.float32),
        jnp.zeros((slot_count, row_count), jnp.float32),
        jnp.zeros((row_count, slot_count, head_dim), jnp.float32),
    )
    running, denominator, weighted = add_piece(
        initial, lax.all_gather(pairs, "row", axis=0, tiled=True), jnp.int32(0)
    )
    return (weighted / denominator.T[..., None], running + jnp.log(denominator))


def attend_back(queries, pairs, seg_all, query_pos, query_seg, log_total, grad_heads, delta):
    head_dim = queries.shape[-1]
    slot_count = queries.shape[1]
    row_count = queries.shape[0]
    score_scale = head_dim ** (-0.5)
    seq_len = pairs.shape[0] * lax.axis_size("row")

    def add_piece(state_now, block_kv, offset):
        key_part = block_kv[..., :head_dim]
        value_part = block_kv[..., head_dim:]
        logits = (
            jnp.einsum("qsd,ksd->sqk", queries, key_part, preferred_element_type=jnp.float32)
            * score_scale
        )
        logits = jnp.where(
            visible(block_kv.shape[0], seg_all, query_pos, query_seg)[None], logits, masked_score
        )
        weights = jnp.exp(logits - log_total[..., None])
        grad_value = jnp.einsum(
            "sqk,qsd->ksd",
            weights.astype(jnp.bfloat16),
            grad_heads,
            preferred_element_type=jnp.float32,
        )
        grad_weights = jnp.einsum(
            "qsd,ksd->sqk", grad_heads, value_part, preferred_element_type=jnp.float32
        )
        grad_logits = (weights * (grad_weights - delta.T[..., None]) * score_scale).astype(
            jnp.bfloat16
        )
        grad_query = jnp.einsum(
            "sqk,ksd->qsd", grad_logits, key_part, preferred_element_type=jnp.float32
        )
        grad_key = jnp.einsum(
            "sqk,qsd->ksd", grad_logits, queries, preferred_element_type=jnp.float32
        )
        grad_pairs = jnp.concatenate([grad_key, grad_value], axis=-1)
        return (grad_query, grad_pairs)

    initial = (
        jnp.zeros((row_count, slot_count, head_dim), jnp.float32),
        jnp.zeros((seq_len, slot_count, 2 * head_dim), jnp.float32),
    )
    grad_query, grad_pairs = add_piece(
        initial, lax.all_gather(pairs, "row", axis=0, tiled=True), jnp.int32(0)
    )
    return (
        grad_query,
        lax.psum_scatter(
            grad_pairs.astype(jnp.bfloat16), "row", scatter_dimension=0, tiled=True
        ).astype(jnp.float32),
    )


def body(
    inputs,
    segment_ids,
    head_map,
    gain_one,
    shift_one,
    gain_two,
    shift_two,
    w_qkv,
    w_out,
    w_up,
    w_down,
    cotangent,
):
    row_tokens = inputs.shape[0]
    slot_count = w_out.shape[1] // HD
    slot_ids = lax.axis_index("col") * slot_count + jnp.arange(slot_count, dtype=jnp.int32)
    in_use = jnp.any(head_map[:, None] == slot_ids[None, :], axis=0).astype(jnp.float32)
    query_pos = lax.axis_index("row") * row_tokens + jnp.arange(row_tokens, dtype=jnp.int32)
    seg_all = lax.all_gather(segment_ids, "row", axis=0, tiled=True)
    stream = inputs
    records = []
    for layer in range(LAYERS):
        normed, standard_one, inverse_one = norm_forward(stream, gain_one[layer], shift_one[layer])
        normed_one = normed.astype(jnp.bfloat16)
        wide_qkv = full_inputs(w_qkv[layer])
        mixed = jnp.dot(normed_one, wide_qkv, preferred_element_type=jnp.float32).astype(
            jnp.bfloat16
        )
        mixed = mixed.reshape(row_tokens, slot_count, 3 * HD)
        queries = mixed[..., :HD]
        pairs = mixed[..., HD:]
        outputs, log_total = attend(queries, pairs, seg_all, query_pos, segment_ids)
        outputs = outputs * in_use[None, :, None]
        heads_low = outputs.astype(jnp.bfloat16).reshape(row_tokens, slot_count * HD)
        wide_out = full_outputs(w_out[layer])
        middle = stream + column_sum(
            jnp.dot(heads_low, wide_out, preferred_element_type=jnp.float32)
        )
        normed, standard_two, inverse_two = norm_forward(middle, gain_two[layer], shift_two[layer])
        normed_two = normed.astype(jnp.bfloat16)
        wide_up = full_inputs(w_up[layer])
        hidden = jnp.dot(normed_two, wide_up, preferred_element_type=jnp.float32)
        active = jax.nn.gelu(hidden, approximate=False).astype(jnp.bfloat16)
        wide_down = full_outputs(w_down[layer])
        stream = middle + column_sum(jnp.dot(active, wide_down, preferred_element_type=jnp.float32))
        kept_blocks = None
        records.append(
            (
                normed_one,
                standard_one,
                inverse_one,
                queries,
                pairs,
                outputs,
                log_total,
                heads_low,
                standard_two,
                inverse_two,
                normed_two,
                hidden,
                active,
                kept_blocks,
            )
        )
    grad = cotangent
    qkv_grads, out_grads, up_grads, down_grads = ([], [], [], [])
    gain_one_parts, shift_one_parts, gain_two_parts, shift_two_parts = ([], [], [], [])
    for layer in reversed(range(LAYERS)):
        (
            normed_one,
            standard_one,
            inverse_one,
            queries,
            pairs,
            outputs,
            log_total,
            heads_low,
            standard_two,
            inverse_two,
            normed_two,
            hidden,
            active,
            kept_blocks,
        ) = records[layer]
        wide_qkv = full_inputs(w_qkv[layer])
        wide_out = full_outputs(w_out[layer])
        wide_up = full_inputs(w_up[layer])
        wide_down = full_outputs(w_down[layer])
        grad_low = grad.astype(jnp.bfloat16)
        share_down = weight_share(grad_low, active)
        grad_active = contract_cols(grad_low, wide_down)
        ignored, pullback = jax.vjp(partial(jax.nn.gelu, approximate=False), hidden)
        grad_hidden = pullback(grad_active)[0].astype(jnp.bfloat16)
        share_up = weight_share(normed_two, grad_hidden)
        incoming = feature_sum(contract_cols(grad_hidden, wide_up))
        back_two, gain_part_two, shift_part_two = norm_backward(
            incoming, standard_two, inverse_two, gain_two[layer]
        )
        grad = grad + back_two
        grad_low = grad.astype(jnp.bfloat16)
        share_out = weight_share(grad_low, heads_low)
        grad_heads = (
            contract_cols(grad_low, wide_out).reshape(row_tokens, slot_count, HD)
            * in_use[None, :, None]
        )
        grad_heads = grad_heads.astype(jnp.bfloat16)
        delta = jnp.sum(grad_heads.astype(jnp.float32) * outputs, axis=-1)
        grad_query, grad_pairs = attend_back(
            queries, pairs, seg_all, query_pos, segment_ids, log_total, grad_heads, delta
        )
        grad_mixed = (
            jnp.concatenate([grad_query, grad_pairs], axis=-1)
            .astype(jnp.bfloat16)
            .reshape(row_tokens, slot_count * 3 * HD)
        )
        share_qkv = weight_share(normed_one, grad_mixed)
        incoming = feature_sum(contract_cols(grad_mixed, wide_qkv))
        back_one, gain_part_one, shift_part_one = norm_backward(
            incoming, standard_one, inverse_one, gain_one[layer]
        )
        grad = grad + back_one
        summed_qkv, summed_out, summed_up, summed_down = finish_layer(
            share_qkv, share_out, share_up, share_down
        )
        qkv_grads.insert(0, summed_qkv)
        out_grads.insert(0, summed_out.T)
        up_grads.insert(0, summed_up)
        down_grads.insert(0, summed_down.T)
        gain_one_parts.insert(0, gain_part_one)
        shift_one_parts.insert(0, shift_part_one)
        gain_two_parts.insert(0, gain_part_two)
        shift_two_parts.insert(0, shift_part_two)
    norm_sums = (
        lax.psum(jnp.stack(gain_one_parts).astype(jnp.bfloat16), ("dp", "row")).astype(jnp.float32),
        lax.psum(jnp.stack(shift_one_parts).astype(jnp.bfloat16), ("dp", "row")).astype(
            jnp.float32
        ),
        lax.psum(jnp.stack(gain_two_parts).astype(jnp.bfloat16), ("dp", "row")).astype(jnp.float32),
        lax.psum(jnp.stack(shift_two_parts).astype(jnp.bfloat16), ("dp", "row")).astype(
            jnp.float32
        ),
    )
    return (
        stream,
        grad,
        norm_sums[0],
        norm_sums[1],
        norm_sums[2],
        norm_sums[3],
        jnp.stack(qkv_grads),
        jnp.stack(out_grads),
        jnp.stack(up_grads),
        jnp.stack(down_grads),
    )


def solution(mesh):
    placed = (
        P(("dp", "row"), None),
        P(("dp", "row")),
        P(),
        P(),
        P(),
        P(),
        P(),
        P(None, "row", "col"),
        P(None, "col", "row"),
        P(None, "row", "col"),
        P(None, "col", "row"),
        P(("dp", "row"), None),
    )
    return jax.shard_map(
        body,
        mesh=mesh,
        in_specs=placed,
        out_specs=(
            P(("dp", "row"), None),
            P(("dp", "row"), None),
            P(),
            P(),
            P(),
            P(),
            P(None, "row", "col"),
            P(None, "col", "row"),
            P(None, "row", "col"),
            P(None, "col", "row"),
        ),
        check_vma=False,
    )
```

profile of v0, /device:TPU:0, one launch (start us, length us, event | category | flops | bytes accessed | tf_op | source)
XLA Modules:
  0.0 1381.6 jit_solution(6639317254432770512)
XLA Ops:
  11.6 31.0 %all-gather.24.cloned.1.call-done = bf16[1,1088,1536]{2,1,0:T(8,128)(2,1)} async-done(((bf16[1,272,1536]{2,1,0:T(8,128)(2,1)}), bf16[1,1088,1536]{2,1,0:T(8,128)(2,1)}) %all-gather.24.cloned.1.call-update) | async-done | bytes 3342352 | tf_op jit(solution)/shard_map/all_gather | solution.py:35
  58.4 27.0 %all-gather.20.cloned.1.call-done = bf16[2048,8,128]{0,2,1:T(8,128)(2,1)} async-done(((bf16[512,8,128]{0,2,1:T(8,128)(2,1)}), bf16[2048,8,128]{0,2,1:T(8,128)(2,1)}) %all-gather.20.cloned.1.call-update) | async-done | bytes 4194320 | tf_op jit(solution)/shard_map/all_gather | solution.py:135
  85.4 15.7 %fusion.181 = (f32[8,512]{1,0:T(8,128)S(1)}, f32[8,512,2048]{2,1,0:T(8,128)}) fusion(bf16[2048,8,128]{0,2,1:T(8,128)(2,1)} %all-gather.20.cloned.1.call-done, bf16[512,8,192]{0,2,1:T(8,128)(2,1)S(1)} %bitcast.192, pred[512,2048]{1,0:T(8,128)(4,1)S(1)} %fusion.19), kind=kOutput, calls=%fused_computation.248 | convolution fusion | flops 1098903552 | bytes 37240832 | tf_op jit(solution)/shard_map/qsd,ksd->sqk/dot_general | solution.py:111
  115.4 15.0 %fusion.182 = (bf16[512,8,64]{0,2,1:T(8,128)(2,1)S(1)}, f32[512,8,64]{0,2,1:T(8,128)}) fusion(f32[8]{0:T(128)S(1)} %convert_element_type.239, f32[512,8]{0,1:T(8,128)S(1)} %bitcast.231, f32[8,512,2048]{2,1,0:T(8,128)} %get-tuple-element.65, f32[8,512]{1,0:T(8,128)S(1)} %broadcast_maximum_fusion.1, bf16[2048,8,128]{0,2,1:T(8,128)(2,1)} %all-gather.20.cloned.1.call-done, ...), kind=kOutput, calls=%fused_computation.249 | convolution fusion | flops 1091567616 | bytes 37273632 | tf_op jit(solution)/shard_map/sqk,ksd->qsd/dot_general | solution.py:121
  138.0 49.8 %all-reduce.14.cloned.1.call-done = bf16[512,1088]{0,1:T(8,128)(2,1)} async-done(((bf16[512,1088]{0,1:T(8,128)(2,1)}), bf16[512,1088]{0,1:T(8,128)(2,1)}) %all-reduce.14.cloned.1.call-update) | async-done | bytes 1114128 | tf_op jit(solution)/shard_map/psum | solution.py:43
  191.8 22.4 %all-gather.28.cloned.1.call-done = bf16[1,1088,1088]{2,1,0:T(8,128)(2,1)} async-done(((bf16[1,272,1088]{2,1,0:T(8,128)(2,1)}), bf16[1,1088,1088]{2,1,0:T(8,128)(2,1)}) %all-gather.28.cloned.1.call-update) | async-done | bytes 2367504 | tf_op jit(solution)/shard_map/all_gather | solution.py:35
  224.2 17.0 %all-gather.30.cloned.1.call-done = bf16[1,1088,1088]{1,2,0:T(8,128)(2,1)} async-done(((bf16[1,1088,272]{1,2,0:T(8,128)(2,1)}), bf16[1,1088,1088]{1,2,0:T(8,128)(2,1)}) %all-gather.30.cloned.1.call-update) | async-done | bytes 2367504 | tf_op jit(solution)/shard_map/all_gather | solution.py:39
  246.6 53.2 %all-reduce.16.cloned.1.call-done = bf16[512,1088]{0,1:T(8,128)(2,1)} async-done(((bf16[512,1088]{0,1:T(8,128)(2,1)}), bf16[512,1088]{0,1:T(8,128)(2,1)}) %all-reduce.16.cloned.1.call-update) | async-done | bytes 1114128 | tf_op jit(solution)/shard_map/psum | solution.py:43
  303.3 27.8 %all-gather.32.cloned.1.call-done = bf16[1,1088,1536]{2,1,0:T(8,128)(2,1)} async-done(((bf16[1,272,1536]{2,1,0:T(8,128)(2,1)}), bf16[1,1088,1536]{2,1,0:T(8,128)(2,1)}) %all-gather.32.cloned.1.call-update) | async-done | bytes 3342352 | tf_op jit(solution)/shard_map/all_gather | solution.py:35
  340.2 33.8 %all-gather.22.cloned.1.call-done = bf16[2048,8,128]{0,2,1:T(8,128)(2,1)} async-done(((bf16[512,8,128]{0,2,1:T(8,128)(2,1)}), bf16[2048,8,128]{0,2,1:T(8,128)(2,1)}) %all-gather.22.cloned.1.call-update) | async-done | bytes 4194320 | tf_op jit(solution)/shard_map/all_gather | solution.py:135
  374.1 15.7 %fusion.183 = (f32[8,512]{1,0:T(8,128)S(1)}, f32[8,512,2048]{2,1,0:T(8,128)}) fusion(bf16[2048,8,128]{0,2,1:T(8,128)(2,1)} %all-gather.22.cloned.1.call-done, bf16[512,8,192]{0,2,1:T(8,128)(2,1)S(1)} %bitcast.195, pred[512,2048]{1,0:T(8,128)(4,1)S(1)} %fusion.19), kind=kOutput, calls=%fused_computation.250 | convolution fusion | flops 1098903552 | bytes 37240832 | tf_op jit(solution)/shard_map/qsd,ksd->sqk/dot_general | solution.py:111
  403.4 15.0 %fusion.184 = (bf16[512,8,64]{0,2,1:T(8,128)(2,1)S(1)}, f32[512,8,64]{0,2,1:T(8,128)}) fusion(f32[8]{0:T(128)S(1)} %convert_element_type.239, f32[512,8]{0,1:T(8,128)S(1)} %bitcast.232, f32[8,512,2048]{2,1,0:T(8,128)} %get-tuple-element.70, f32[8,512]{1,0:T(8,128)S(1)} %broadcast_maximum_fusion, bf16[2048,8,128]{0,2,1:T(8,128)(2,1)} %all-gather.22.cloned.1.call-done, ...), kind=kOutput, calls=%fused_computation.251 | convolution fusion | flops 1091567616 | bytes 37273632 | tf_op jit(solution)/shard_map/sqk,ksd->qsd/dot_general | solution.py:121
  424.4 51.3 %all-reduce.18.cloned.1.call-done = bf16[512,1088]{0,1:T(8,128)(2,1)} async-done(((bf16[512,1088]{0,1:T(8,128)(2,1)}), bf16[512,1088]{0,1:T(8,128)(2,1)}) %all-reduce.18.cloned.1.call-update) | async-done | bytes 1114128 | tf_op jit(solution)/shard_map/psum | solution.py:43
  478.8 23.4 %all-gather.36.cloned.1.call-done = bf16[1,1088,1088]{2,1,0:T(8,128)(2,1)} async-done(((bf16[1,272,1088]{2,1,0:T(8,128)(2,1)}), bf16[1,1088,1088]{2,1,0:T(8,128)(2,1)}) %all-gather.36.cloned.1.call-update) | async-done | bytes 2367504 | tf_op jit(solution)/shard_map/all_gather | solution.py:35
  512.0 16.8 %all-gather.38.cloned.1.call-done = bf16[1,1088,1088]{1,2,0:T(8,128)(2,1)} async-done(((bf16[1,1088,272]{1,2,0:T(8,128)(2,1)}), bf16[1,1088,1088]{1,2,0:T(8,128)(2,1)}) %all-gather.38.cloned.1.call-update) | async-done | bytes 2367504 | tf_op jit(solution)/shard_map/all_gather | solution.py:39
  537.5 53.7 %all-reduce.20.cloned.1.call-done = bf16[512,1088]{0,1:T(8,128)(2,1)} async-done(((bf16[512,1088]{0,1:T(8,128)(2,1)}), bf16[512,1088]{0,1:T(8,128)(2,1)}) %all-reduce.20.cloned.1.call-update) | async-done | bytes 1114128 | tf_op jit(solution)/shard_map/psum | solution.py:47
  597.5 14.8 %fusion.61 = bf16[2048,8,64]{0,2,1:T(8,128)(2,1)} fusion(bf16[512,8,64]{0,2,1:T(8,128)(2,1)S(1)} %get-tuple-element.41, f32[8,512,2048]{2,1,0:T(8,128)} %get-tuple-element.70, f32[8,512]{1,0:T(8,128)S(1)} %get-tuple-element.62), kind=kOutput, calls=%fused_computation.82 | convolution fusion | flops 1091567616 | bytes 36192256 | tf_op jit(solution)/shard_map/sqk,qsd->ksd/dot_general | solution.py:158
  612.3 15.4 %multiply_convert_fusion.1 = bf16[8,512,2048]{2,1,0:T(8,128)(2,1)S(1)} fusion(f32[8,512,2048]{2,1,0:T(8,128)} %get-tuple-element.70, bf16[512,8,64]{0,2,1:T(8,128)(2,1)S(1)} %get-tuple-element.41, f32[8,512]{1,0:T(8,128)S(1)} %bitcast.230, f32[8,512]{1,0:T(8,128)S(1)} %get-tuple-element.62, bf16[2048,8,128]{0,2,1:T(8,128)(2,1)} %all-gather.22.cloned.1.call-done), kind=kOutput, calls=%fused_computation.2 | convolution fusion | flops 1115684864 | bytes 52985856 | tf_op jit(solution)/shard_map/qsd,ksd->sqk/dot_general | solution.py:164
  649.9 31.2 %reduce-scatter.19.cloned.1.call-done = bf16[512,8,128]{0,2,1:T(8,128)(2,1)} async-done(((bf16[2048,8,128]{0,2,1:T(8,128)(2,1)}), bf16[512,8,128]{0,2,1:T(8,128)(2,1)}) %reduce-scatter.19.cloned.1.call-update) | async-done | bytes 1048592 | tf_op jit(solution)/shard_map/reduce_scatter | solution.py:188
  688.0 54.0 %all-reduce.22.cloned.1.call-done = bf16[512,1088]{0,1:T(8,128)(2,1)} async-done(((bf16[512,1088]{0,1:T(8,128)(2,1)}), bf16[512,1088]{0,1:T(8,128)(2,1)}) %all-reduce.22.cloned.1.call-update) | async-done | bytes 1114128 | tf_op jit(solution)/shard_map/psum | solution.py:47
  755.2 53.2 %all-reduce.24.cloned.1.call-done = bf16[512,1088]{0,1:T(8,128)(2,1)} async-done(((bf16[512,1088]{0,1:T(8,128)(2,1)}), bf16[512,1088]{0,1:T(8,128)(2,1)}) %all-reduce.24.cloned.1.call-update) | async-done | bytes 1114128 | tf_op jit(solution)/shard_map/psum | solution.py:47
  814.2 14.8 %fusion.58 = bf16[2048,8,64]{0,2,1:T(8,128)(2,1)} fusion(bf16[512,8,64]{0,2,1:T(8,128)(2,1)S(1)} %get-tuple-element.37, f32[8,512,2048]{2,1,0:T(8,128)} %get-tuple-element.65, f32[8,512]{1,0:T(8,128)S(1)} %copy-done.48), kind=kOutput, calls=%fused_computation.81 | convolution fusion | flops 1091567616 | bytes 36192256 | tf_op jit(solution)/shard_map/sqk,qsd->ksd/dot_general | solution.py:158
  829.0 15.5 %multiply_convert_fusion = bf16[8,512,2048]{2,1,0:T(8,128)(2,1)S(1)} fusion(f32[8,512,2048]{2,1,0:T(8,128)} %get-tuple-element.65, bf16[512,8,64]{0,2,1:T(8,128)(2,1)S(1)} %get-tuple-element.37, f32[8,512]{1,0:T(8,128)S(1)} %bitcast.229, f32[8,512]{1,0:T(8,128)S(1)} %copy-done.48, bf16[2048,8,128]{0,2,1:T(8,128)(2,1)} %all-gather.20.cloned.1.call-done), kind=kOutput, calls=%fused_computation | convolution fusion | flops 1115684864 | bytes 52985856 | tf_op jit(solution)/shard_map/qsd,ksd->sqk/dot_general | solution.py:164
  912.7 24.8 %reduce-scatter.29.cloned.1.call-done = bf16[136,512]{1,0:T(8,128)(2,1)} async-done(((bf16[1088,512]{1,0:T(8,128)(2,1)}), bf16[136,512]{1,0:T(8,128)(2,1)}) %reduce-scatter.29.cloned.1.call-update) | async-done | bytes 139280 | tf_op jit(solution)/shard_map/reduce_scatter | solution.py:70
  948.6 35.1 %reduce-scatter.37.cloned.1.call-done = bf16[136,1088]{1,0:T(8,128)(2,1)} async-done(((bf16[1088,1088]{1,0:T(8,128)(2,1)}), bf16[136,1088]{1,0:T(8,128)(2,1)}) %reduce-scatter.37.cloned.1.call-update) | async-done | bytes 295952
  993.8 37.1 %reduce-scatter.33.cloned.1.call-done = bf16[136,1088]{1,0:T(8,128)(2,1)} async-done(((bf16[1088,1088]{1,0:T(8,128)(2,1)}), bf16[136,1088]{1,0:T(8,128)(2,1)}) %reduce-scatter.33.cloned.1.call-update) | async-done | bytes 295952
  1043.0 27.7 %reduce-scatter.27.cloned.1.call-done = bf16[136,512]{1,0:T(8,128)(2,1)} async-done(((bf16[1088,512]{1,0:T(8,128)(2,1)}), bf16[136,512]{1,0:T(8,128)(2,1)}) %reduce-scatter.27.cloned.1.call-update) | async-done | bytes 139280 | tf_op jit(solution)/shard_map/reduce_scatter | solution.py:70
  1077.9 39.9 %reduce-scatter.31.cloned.1.call-done = bf16[136,1088]{1,0:T(8,128)(2,1)} async-done(((bf16[1088,1088]{1,0:T(8,128)(2,1)}), bf16[136,1088]{1,0:T(8,128)(2,1)}) %reduce-scatter.31.cloned.1.call-update) | async-done | bytes 295952
  1129.3 35.0 %reduce-scatter.35.cloned.1.call-done = bf16[136,1088]{1,0:T(8,128)(2,1)} async-done(((bf16[1088,1088]{1,0:T(8,128)(2,1)}), bf16[136,1088]{1,0:T(8,128)(2,1)}) %reduce-scatter.35.cloned.1.call-update) | async-done | bytes 295952
  1177.6 37.8 %reduce-scatter.25.cloned.1.call-done = bf16[136,1536]{1,0:T(8,128)(2,1)} async-done(((bf16[1088,1536]{1,0:T(8,128)(2,1)}), bf16[136,1536]{1,0:T(8,128)(2,1)}) %reduce-scatter.25.cloned.1.call-update) | async-done | bytes 417808 | tf_op jit(solution)/shard_map/reduce_scatter | solution.py:70
  1229.2 81.0 %all-reduce.26.cloned.1.call-done = (bf16[512,1088]{0,1:T(8,128)(2,1)}, bf16[512,1088]{0,1:T(8,128)(2,1)}) async-done(((bf16[512,1088]{0,1:T(8,128)(2,1)}, bf16[512,1088]{0,1:T(8,128)(2,1)}), (bf16[512,1088]{0,1:T(8,128)(2,1)}, bf16[512,1088]{0,1:T(8,128)(2,1)})) %all-reduce.26.cloned.1.call-update) | async-done | bytes 2228240 | tf_op jit(solution)/shard_map/psum | solution.py:43
  1314.9 24.1 %all-reduce.4 = (bf16[2,1088]{1,0:T(2,128)(2,1)S(1)}, bf16[2,1088]{1,0:T(2,128)(2,1)S(1)}, bf16[2,1088]{1,0:T(2,128)(2,1)S(1)}, bf16[2,1088]{1,0:T(2,128)(2,1)S(1)}) all-reduce(bf16[2,1088]{1,0:T(2,128)(2,1)S(1)} %pad_maximum_fusion.2, ...), channel_id=1, replica_groups=mesh['dp'=2,'row'=4,'col'=4] {'dp','row'}, use_global_device_ids=true, to_apply=%region_35.36 | all-reduce | flops 8704 | bytes 34816 | tf_op jit(solution)/shard_map/psum | solution.py:328
  (368 shorter events, 355.7 us)
Async XLA Ops:
  7.2 35.4 %all-gather.24.cloned.1.call-start = ((), (), s32[]{:S(2)}) async-start(), calls=%async_computation.24 | async-start | bytes 4177920 | tf_op jit(solution)/shard_map/all_gather | solution.py:35
  10.1 75.3 %all-gather.20.cloned.1.call-start = ((), (), s32[]{:S(2)}) async-start(), calls=%async_computation.10 | async-start | bytes 5242880 | tf_op jit(solution)/shard_map/all_gather | solution.py:135
  50.8 79.6 %all-gather.26.cloned.1.call-start = ((), (), s32[]{:S(2)}) async-start(), calls=%async_computation.25 | async-start | bytes 1392640 | tf_op jit(solution)/shard_map/all_gather | solution.py:39
  52.0 135.7 %all-reduce.14.cloned.1.call-start = ((), (), s32[]{:S(2)}) async-start(), calls=%async_computation.11 | async-start | bytes 2228224 | tf_op jit(solution)/shard_map/psum | solution.py:43
  133.6 80.5 %all-gather.28.cloned.1.call-start = ((), (), s32[]{:S(2)}) async-start(), calls=%async_computation.26 | async-start | bytes 3133440 | tf_op jit(solution)/shard_map/all_gather | solution.py:35
  134.9 106.3 %all-gather.30.cloned.1.call-start = ((), (), s32[]{:S(2)}) async-start(), calls=%async_computation.27 | async-start | bytes 3133440 | tf_op jit(solution)/shard_map/all_gather | solution.py:39
  137.3 162.5 %all-reduce.16.cloned.1.call-start = ((), (), s32[]{:S(2)}) async-start(), calls=%async_computation.12 | async-start | bytes 2228224 | tf_op jit(solution)/shard_map/psum | solution.py:43
  190.1 109.8 %copy-start.2 = (f32[512,1088]{0,1:T(8,128)}, f32[512,1088]{0,1:T(8,128)S(1)}, u32[]{:S(2)}) copy-start(f32[512,1088]{0,1:T(8,128)S(1)} %get-tuple-element.51) | copy-start | bytes 6684676
  245.8 85.3 %all-gather.32.cloned.1.call-start = ((), (), s32[]{:S(2)}) async-start(), calls=%async_computation.28 | async-start | bytes 4177920 | tf_op jit(solution)/shard_map/all_gather | solution.py:35
  246.6 127.5 %all-gather.22.cloned.1.call-start = ((), (), s32[]{:S(2)}) async-start(), calls=%async_computation.13 | async-start | bytes 5242880 | tf_op jit(solution)/shard_map/all_gather | solution.py:135
  339.4 79.0 %all-gather.34.cloned.1.call-start = ((), (), s32[]{:S(2)}) async-start(), calls=%async_computation.29 | async-start | bytes 1392640 | tf_op jit(solution)/shard_map/all_gather | solution.py:39
  340.0 135.7 %all-reduce.18.cloned.1.call-start = ((), (), s32[]{:S(2)}) async-start(), calls=%async_computation.14 | async-start | bytes 2228224 | tf_op jit(solution)/shard_map/psum | solution.py:43
  421.7 80.5 %all-gather.36.cloned.1.call-start = ((), (), s32[]{:S(2)}) async-start(), calls=%async_computation.30 | async-start | bytes 3133440 | tf_op jit(solution)/shard_map/all_gather | solution.py:35
  422.3 106.5 %all-gather.38.cloned.1.call-start = ((), (), s32[]{:S(2)}) async-start(), calls=%async_computation.31 | async-start | bytes 3133440 | tf_op jit(solution)/shard_map/all_gather | solution.py:39
  423.0 168.2 %all-reduce.20.cloned.1.call-start = ((), (), s32[]{:S(2)}) async-start(), calls=%async_computation.15 | async-start | bytes 2228224 | tf_op jit(solution)/shard_map/psum | solution.py:47
  478.1 116.2 %copy-start.5 = (f32[512,1088]{0,1:T(8,128)}, f32[512,1088]{0,1:T(8,128)S(1)}, u32[]{:S(2)}) copy-start(f32[512,1088]{0,1:T(8,128)S(1)} %get-tuple-element.45) | copy-start | bytes 6684676
  537.2 143.8 %reduce-scatter.19.cloned.1.call-start = ((), (), s32[]{:S(2)}) async-start(), calls=%async_computation.16 | async-start | bytes 5242880 | tf_op jit(solution)/shard_map/reduce_scatter | solution.py:188
  637.0 105.0 %all-reduce.22.cloned.1.call-start = ((), (), s32[]{:S(2)}) async-start(), calls=%async_computation.17 | async-start | bytes 2228224 | tf_op jit(solution)/shard_map/psum | solution.py:47
  687.9 120.5 %all-reduce.24.cloned.1.call-start = ((), (), s32[]{:S(2)}) async-start(), calls=%async_computation.18 | async-start | bytes 2228224 | tf_op jit(solution)/shard_map/psum | solution.py:47
  755.0 148.3 %reduce-scatter.21.cloned.1.call-start = ((), (), s32[]{:S(2)}) async-start(), calls=%async_computation.19 | async-start | bytes 5242880 | tf_op jit(solution)/shard_map/reduce_scatter | solution.py:188
  853.5 83.9 %reduce-scatter.29.cloned.1.call-start = ((), (), s32[]{:S(2)}) async-start(), calls=%async_computation.23 | async-start | bytes 1253376 | tf_op jit(solution)/shard_map/reduce_scatter | solution.py:70
  856.7 127.1 %reduce-scatter.37.cloned.1.call-start = ((), (), s32[]{:S(2)}) async-start(), calls=%async_computation.35 | async-start | bytes 2820096
  863.3 167.6 %reduce-scatter.33.cloned.1.call-start = ((), (), s32[]{:S(2)}) async-start(), calls=%async_computation.33 | async-start | bytes 2820096
  868.1 202.6 %reduce-scatter.27.cloned.1.call-start = ((), (), s32[]{:S(2)}) async-start(), calls=%async_computation.22 | async-start | bytes 1253376 | tf_op jit(solution)/shard_map/reduce_scatter | solution.py:70
  871.3 246.5 %reduce-scatter.31.cloned.1.call-start = ((), (), s32[]{:S(2)}) async-start(), calls=%async_computation.32 | async-start | bytes 2820096
  875.9 288.3 %reduce-scatter.35.cloned.1.call-start = ((), (), s32[]{:S(2)}) async-start(), calls=%async_computation.34 | async-start | bytes 2820096
  880.6 334.8 %reduce-scatter.25.cloned.1.call-start = ((), (), s32[]{:S(2)}) async-start(), calls=%async_computation.21 | async-start | bytes 3760128 | tf_op jit(solution)/shard_map/reduce_scatter | solution.py:70
  886.0 424.1 %all-reduce.26.cloned.1.call-start = ((), (), s32[]{:S(2)}) async-start(), calls=%async_computation.36 | async-start | bytes 4456448 | tf_op jit(solution)/shard_map/psum | solution.py:43
  910.8 449.4 %reduce-scatter.23.cloned.1.call-start = ((), (), s32[]{:S(2)}) async-start(), calls=%async_computation.20 | async-start | bytes 3760128 | tf_op jit(solution)/shard_map/reduce_scatter | solution.py:70
  1176.0 135.9 %copy-start.58 = (f32[1088]{0:T(1024)S(1)}, f32[1088]{0:T(1024)}, u32[]{:S(2)}) copy-start(f32[1088]{0:T(1024)} %copy-done.57) | copy-start | bytes 13060
  1176.0 135.9 %copy-start.64 = (f32[512]{0:T(512)S(1)}, f32[512]{0:T(512)}, u32[]{:S(2)}) copy-start(f32[512]{0:T(512)} %copy-done.63) | copy-start | bytes 6148
  1176.0 135.9 %copy-start.66 = (f32[512]{0:T(512)S(1)}, f32[512]{0:T(512)}, u32[]{:S(2)}) copy-start(f32[512]{0:T(512)} %copy-done.65) | copy-start | bytes 6148
  (82 other events, 1116.2 us)
Sparse Core Ops, SparseCore 0:
  10.2 32.3 all-gather.23
  50.9 34.4 all-gather.19
  87.6 17.0 all-gather.25
  133.8 53.9 all-reduce.13
  189.8 24.3 all-gather.27
  216.3 24.9 all-gather.29
  246.0 53.8 all-reduce.15
  302.0 29.1 all-gather.31
  339.6 34.4 all-gather.21
  375.5 17.0 all-gather.33
  421.8 53.9 all-reduce.17
  477.8 24.3 all-gather.35
  503.9 24.8 all-gather.37
  537.4 53.8 all-reduce.19
  637.1 43.9 reduce-scatter.18
  688.0 53.8 all-reduce.21
  755.1 53.3 all-reduce.23
  853.6 43.9 reduce-scatter.20
  900.9 36.5 reduce-scatter.28
  940.7 43.0 reduce-scatter.36
  987.8 43.0 reduce-scatter.32
  1034.1 36.5 reduce-scatter.26
  1074.7 43.0 reduce-scatter.30
  1121.1 43.0 reduce-scatter.34
  1168.2 47.1 reduce-scatter.24
  1218.4 91.6 all-reduce.25
  1313.9 46.2 reduce-scatter.22
where the time goes:
time: 1390 us; the launch traced here: 1380 us
  waiting for transfers between devices  878 us (63%)
  matrix products  250 us (18%)
  blocking collectives  111 us (8%)
  other arithmetic  84.7 us (6%)
  local copies, waits for them, and re-layouts  38.7 us (3%)
  between operations  16 us (1%)
    psum x4, waiting for transfers between devices, column_sum(): return lax.psum(pieces.astype(jnp.bfloat16), 'col').astype(jnp.float32)  235 us
    psum x3, waiting for transfers between devices, feature_sum(): return lax.psum(pieces.astype(jnp.bfloat16), 'col').astype(jnp.float32)  161 us
    unnamed x31, waiting for transfers between devices  150 us
    all_gather x4, waiting for transfers between devices, full_inputs(): return lax.all_gather(shard, 'row', axis=0, tiled=True)  105 us
    reduce_scatter x4, waiting for transfers between devices, weight_share(): lax.psum_scatter(contract_rows(reordered, right).astype(jnp.bfloat16), ('...  101 us
    all_gather x2, waiting for transfers between devices, attend(): lax.all_gather(pairs, 'row', axis=0, tiled=True)  60.8 us
    all_gather x4, waiting for transfers between devices, full_outputs(): return lax.all_gather(shard, 'row', axis=1, tiled=True)  33.8 us
    dot_general x2, matrix products, add_piece(): jnp.einsum('qsd,ksd->sqk', queries, key_part, preferred_element_type=jnp....  31.4 us
  transfers between devices with their start and end apart: 27, of which 24 were waited for; matrix products, arithmetic and copies ran while one was open for 15% of the time, Pallas kernels for 0%

commit v1 on v0

v1 whole, which is shorter than its diff:
```python
from functools import partial

import jax
import jax.numpy as jnp
from jax import lax
from jax.experimental import pallas as pl
from jax.experimental.pallas import tpu as pltpu
from jax.sharding import PartitionSpec as P

HD = 64
LAYERS = 2


norm_eps = 1e-05
masked_score = -1e30
start_score = -1e20


def norm_forward(stream, scales, shifts):
    centre = stream - jnp.mean(stream, axis=-1, keepdims=True)
    inverse = lax.rsqrt(jnp.mean(centre * centre, axis=-1, keepdims=True) + norm_eps)
    standard = centre * inverse
    return (standard * scales + shifts, standard, inverse)


def norm_backward(incoming, standard, inverse, scales):
    scaled = incoming * scales
    grad_stream = inverse * (
        scaled
        - jnp.mean(scaled, axis=-1, keepdims=True)
        - standard * jnp.mean(scaled * standard, axis=-1, keepdims=True)
    )
    return (grad_stream, jnp.sum(incoming * standard, axis=0), jnp.sum(incoming, axis=0))


def swap(value, axis, bit):
    count = lax.axis_size(axis)
    return lax.ppermute(value, axis, [(i, i ^ bit) for i in range(count)])


def gather_rows(shard):
    count = lax.axis_size("row")
    me = lax.axis_index("row")
    held = shard
    bit, done = count // 2, 0
    while bit:
        other = swap(held, "row", bit)
        upper = (me & bit) != 0
        held = jnp.stack(
            [jnp.where(upper, other, held), jnp.where(upper, held, other)], axis=done
        )
        bit, done = bit // 2, done + 1
    return held.reshape((count * shard.shape[0],) + shard.shape[1:])


def everyone_sum(pieces):
    for axis in ("row", "dp"):
        bit = 1
        while bit < lax.axis_size(axis):
            pieces = pieces + swap(pieces, axis, bit)
            bit *= 2
    return pieces


def column_sum(pieces):
    return lax.psum(pieces.astype(jnp.bfloat16), "col").astype(jnp.float32)


def contract_rows(left, right):
    return lax.dot_general(
        left, right, (((0,), (0,)), ((), ())), preferred_element_type=jnp.float32
    )


def contract_cols(left, right):
    return lax.dot_general(
        left, right, (((1,), (1,)), ((), ())), preferred_element_type=jnp.float32
    )


class Share:
    def __init__(self, left, right, right_dim=0):
        row_count = lax.axis_size("row")
        tokens_here, width = left.shape
        self.piece = width // row_count

        def product(part):
            return lax.dot_general(
                part, right, (((0,), (right_dim,)), ((), ())), preferred_element_type=jnp.float32
            )

        halves = left.reshape(tokens_here, row_count // 2, 2, self.piece)
        even = halves[:, :, 0].reshape(tokens_here, width // 2)
        odd = halves[:, :, 1].reshape(tokens_here, width // 2)
        upper = (lax.axis_index("row") & 1) != 0
        self.give = product(jnp.where(upper, even, odd)).astype(jnp.bfloat16)
        self.total = product(jnp.where(upper, odd, even))
        self.steps = [("row", 1 << i) for i in range((row_count - 1).bit_length())]
        self.steps += [("dp", 1 << i) for i in range((lax.axis_size("dp") - 1).bit_length())]

    def begin(self):
        axis, bit = self.steps.pop(0)
        return swap(self.give, axis, bit)

    def finish(self, sent):
        total = self.total + sent.astype(jnp.float32)
        if self.steps and self.steps[0][0] == "row":
            total = total.reshape(-1, 2, self.piece, total.shape[-1])
            upper = (lax.axis_index("row") & self.steps[0][1]) != 0
            self.give = jnp.where(upper, total[:, 0], total[:, 1]).astype(jnp.bfloat16)
            self.give = self.give.reshape(-1, total.shape[-1])
            total = jnp.where(upper, total[:, 1], total[:, 0])
            total = total.reshape(-1, total.shape[-1])
        elif self.steps:
            self.give = total.astype(jnp.bfloat16)
            total = self.give.astype(jnp.float32)
        self.total = total

    def result(self):
        while self.steps:
            self.finish(self.begin())
        return self.total


def beside(value, *shares):
    shares = [share for share in shares if share.steps]
    sent = [share.begin() for share in shares]
    value, *sent = lax.optimization_barrier((value, *sent))
    for share, part in zip(shares, sent):
        share.finish(part)
    return value


def kept(block, tokens_here, low_edge, query_pos):
    key_pos = block * tokens_here + lax.broadcasted_iota(jnp.int32, (tokens_here, tokens_here), 0)
    return (key_pos >= low_edge) & (key_pos <= query_pos)


def attend_kernel(place, used, edge, query, pairs, out, out_low, log_total):
    tokens_here = query.shape[0]
    head_dim = out.shape[0]
    row = place[0]
    queries = query[...]
    low_edge = edge[...]
    query_pos = row * tokens_here + lax.broadcasted_iota(jnp.int32, (1, tokens_here), 1)

    def step(block, state):
        running, denominator, weighted = state
        part = pairs[pl.ds(pl.multiple_of(block * tokens_here, tokens_here), tokens_here), :]
        logits = contract_cols(part, queries)
        logits = jnp.where(
            kept(block, tokens_here, low_edge, query_pos), logits, masked_score
        )
        newest = jnp.maximum(running, jnp.max(logits, axis=0, keepdims=True))
        factor = jnp.exp(running - newest)
        weights = jnp.exp(logits - newest)
        denominator = denominator * factor + jnp.sum(weights, axis=0, keepdims=True)
        weighted = weighted * factor + contract_rows(part, weights.astype(jnp.bfloat16))
        return (newest, denominator, weighted)

    running, denominator, weighted = lax.fori_loop(
        0,
        row + 1,
        step,
        (
            jnp.full((1, tokens_here), start_score, jnp.float32),
            jnp.zeros((1, tokens_here), jnp.float32),
            jnp.zeros((2 * head_dim, tokens_here), jnp.float32),
        ),
    )
    scale = used[pl.program_id(0)].astype(jnp.float32) / denominator
    result = weighted[head_dim:] * scale
    out[...] = result
    out_low[...] = result.astype(jnp.bfloat16)
    log_total[...] = running + jnp.log(denominator)


def back_kernel(place, edge, query, grads, pairs, out, log_total, grad_query, grad_pairs):
    tokens_here = query.shape[0]
    head_dim = out.shape[0]
    row = place[0]
    queries = query[...]
    grad_heads = grads[...]
    low_edge = edge[...]
    logs = log_total[...]
    query_pos = row * tokens_here + lax.broadcasted_iota(jnp.int32, (1, tokens_here), 1)
    turned = grad_heads.astype(jnp.float32).T
    delta = jnp.sum(turned[head_dim:] * out[...], axis=0, keepdims=True)

    def step(block, total):
        here = pl.ds(pl.multiple_of(block * tokens_here, tokens_here), tokens_here)
        part = pairs[here, :]
        logits = contract_cols(part, queries)
        logits = jnp.where(
            kept(block, tokens_here, low_edge, query_pos), logits, masked_score
        )
        weights = jnp.exp(logits - logs)
        grad_weights = contract_cols(part, grad_heads)
        grad_logits = (weights * (grad_weights - delta)).astype(jnp.bfloat16)
        grad_pairs[here, :] = (
            jnp.dot(grad_logits, queries, preferred_element_type=jnp.float32)
            + jnp.dot(
                weights.astype(jnp.bfloat16), grad_heads, preferred_element_type=jnp.float32
            )
        ).astype(jnp.bfloat16)
        return total + contract_rows(part, grad_logits)

    total = lax.fori_loop(
        0, row + 1, step, jnp.zeros((2 * head_dim, tokens_here), jnp.float32)
    )
    grad_query[...] = (total.T * head_dim ** (-0.5)).astype(jnp.bfloat16)

    def clear(block, carry):
        here = pl.ds(pl.multiple_of(block * tokens_here, tokens_here), tokens_here)
        grad_pairs[here, :] = jnp.zeros((tokens_here, 2 * head_dim), jnp.bfloat16)
        return carry

    lax.fori_loop(row + 1, pairs.shape[0] // tokens_here, clear, 0)


def attend(place, used, edge, query, pairs):
    tokens_here, wide = query.shape
    slots = wide // (2 * HD)
    count = pairs.shape[0]
    scalar = pl.BlockSpec(memory_space=pltpu.SMEM)
    return pl.pallas_call(
        attend_kernel,
        grid=(slots,),
        in_specs=[
            scalar,
            scalar,
            pl.BlockSpec((1, tokens_here), lambda s: (0, 0)),
            pl.BlockSpec((tokens_here, 2 * HD), lambda s: (0, s)),
            pl.BlockSpec((count, 2 * HD), lambda s: (0, s)),
        ],
        out_specs=[
            pl.BlockSpec((None, HD, tokens_here), lambda s: (s, 0, 0)),
            pl.BlockSpec((None, HD, tokens_here), lambda s: (s, 0, 0)),
            pl.BlockSpec((None, 1, tokens_here), lambda s: (s, 0, 0)),
        ],
        out_shape=[
            jax.ShapeDtypeStruct((slots, HD, tokens_here), jnp.float32),
            jax.ShapeDtypeStruct((slots, HD, tokens_here), jnp.bfloat16),
            jax.ShapeDtypeStruct((slots, 1, tokens_here), jnp.float32),
        ],
        compiler_params=pltpu.CompilerParams(vmem_limit_bytes=32 * 1024 * 1024),
        cost_estimate=pl.CostEstimate(
            flops=8 * slots * tokens_here * count * 4 * HD,
            bytes_accessed=4 * pairs.size,
            transcendentals=slots * tokens_here * count,
        ),
    )(place, used, edge, query, pairs)


def attend_back(place, edge, query, grads, pairs, out, log_total):
    tokens_here, wide = query.shape
    slots = wide // (2 * HD)
    count = pairs.shape[0]
    scalar = pl.BlockSpec(memory_space=pltpu.SMEM)
    own = pl.BlockSpec((tokens_here, 2 * HD), lambda s: (0, s))
    every = pl.BlockSpec((count, 2 * HD), lambda s: (0, s))
    return pl.pallas_call(
        back_kernel,
        grid=(slots,),
        in_specs=[
            scalar,
            pl.BlockSpec((1, tokens_here), lambda s: (0, 0)),
            own,
            own,
            every,
            pl.BlockSpec((None, HD, tokens_here), lambda s: (s, 0, 0)),
            pl.BlockSpec((None, 1, tokens_here), lambda s: (s, 0, 0)),
        ],
        out_specs=[own, every],
        out_shape=[
            jax.ShapeDtypeStruct(query.shape, jnp.bfloat16),
            jax.ShapeDtypeStruct(pairs.shape, jnp.bfloat16),
        ],
        compiler_params=pltpu.CompilerParams(vmem_limit_bytes=32 * 1024 * 1024),
        cost_estimate=pl.CostEstimate(
            flops=16 * slots * tokens_here * count * 4 * HD,
            bytes_accessed=6 * pairs.size,
            transcendentals=slots * tokens_here * count,
        ),
    )(place, edge, query, grads, pairs, out, log_total)


def body(
    inputs,
    segment_ids,
    head_map,
    gain_one,
    shift_one,
    gain_two,
    shift_two,
    w_qkv,
    w_out,
    w_up,
    w_down,
    cotangent,
):
    row_tokens = inputs.shape[0]
    slot_count = w_out.shape[1] // HD
    slot_ids = lax.axis_index("col") * slot_count + jnp.arange(slot_count, dtype=jnp.int32)
    used = jnp.any(head_map[:, None] == slot_ids[None, :], axis=0)
    in_use = used.astype(jnp.float32)
    used = used.astype(jnp.int32)
    place = lax.axis_index("row").reshape(1).astype(jnp.int32)
    seg_all = gather_rows(segment_ids)
    edge = jnp.sum(
        (seg_all[:, None] < segment_ids[None, :]).astype(jnp.int32), axis=0, keepdims=True
    )
    wide = []
    for layer in range(LAYERS):
        wide.append(
            (
                gather_rows(w_qkv[layer]),
                gather_rows(w_out[layer].T),
                gather_rows(w_up[layer]),
                gather_rows(w_down[layer].T),
            )
        )
    stream = inputs
    records = []
    for layer in range(LAYERS):
        wide_qkv, wide_out, wide_up, wide_down = wide[layer]
        normed, standard_one, inverse_one = norm_forward(stream, gain_one[layer], shift_one[layer])
        normed_one = normed.astype(jnp.bfloat16)
        mixed = jnp.dot(normed_one, wide_qkv, preferred_element_type=jnp.float32).astype(
            jnp.bfloat16
        )
        mixed = mixed.reshape(row_tokens, slot_count, 3 * HD)
        pairs = lax.all_gather(
            mixed[..., HD:].reshape(row_tokens, slot_count * 2 * HD), "row", axis=0, tiled=True
        )
        query = jnp.pad(mixed[..., :HD] * HD ** (-0.5), ((0, 0), (0, 0), (0, HD)))
        query = query.reshape(row_tokens, slot_count * 2 * HD)
        outputs, heads_low, log_total = attend(place, used, edge, query, pairs)
        heads_low = heads_low.reshape(slot_count * HD, row_tokens)
        middle = stream + column_sum(
            lax.dot_general(
                heads_low, wide_out, (((0,), (1,)), ((), ())), preferred_element_type=jnp.float32
            )
        )
        normed, standard_two, inverse_two = norm_forward(middle, gain_two[layer], shift_two[layer])
        normed_two = normed.astype(jnp.bfloat16)
        hidden = jnp.dot(normed_two, wide_up, preferred_element_type=jnp.float32)
        active = jax.nn.gelu(hidden, approximate=False).astype(jnp.bfloat16)
        branch = contract_cols(active, wide_down)
        if layer < LAYERS - 1:
            stream = middle + column_sum(branch)
        else:
            branch = branch.astype(jnp.bfloat16)
        records.append(
            (
                normed_one,
                standard_one,
                inverse_one,
                query,
                pairs,
                outputs,
                log_total,
                heads_low,
                standard_two,
                inverse_two,
                normed_two,
                hidden,
                active,
            )
        )
    grad = cotangent
    shares = [None] * LAYERS
    late = ()
    norm_grads = [None] * LAYERS
    for layer in reversed(range(LAYERS)):
        (
            normed_one,
            standard_one,
            inverse_one,
            query,
            pairs,
            outputs,
            log_total,
            heads_low,
            standard_two,
            inverse_two,
            normed_two,
            hidden,
            active,
        ) = records[layer]
        wide_qkv, wide_out, wide_up, wide_down = wide[layer]
        grad_low = grad.astype(jnp.bfloat16)
        grad_active = jnp.dot(grad_low, wide_down, preferred_element_type=jnp.float32)
        ignored, pullback = jax.vjp(partial(jax.nn.gelu, approximate=False), hidden)
        grad_hidden = pullback(grad_active)[0].astype(jnp.bfloat16)
        incoming = column_sum(contract_cols(grad_hidden, wide_up))
        share_down = Share(grad_low, active)
        share_up = Share(normed_two, grad_hidden)
        incoming = beside(incoming, share_down, share_up, *late)
        back_two, gain_part_two, shift_part_two = norm_backward(
            incoming, standard_two, inverse_two, gain_two[layer]
        )
        grad = grad + back_two
        grad_low = grad.astype(jnp.bfloat16)
        grad_heads = (
            jnp.dot(grad_low, wide_out, preferred_element_type=jnp.float32).reshape(
                row_tokens, slot_count, HD
            )
            * in_use[None, :, None]
        )
        grad_heads = jnp.pad(grad_heads.astype(jnp.bfloat16), ((0, 0), (0, 0), (HD, 0)))
        grad_heads = grad_heads.reshape(row_tokens, slot_count * 2 * HD)
        if layer == LAYERS - 1:
            branch, grad_heads = lax.optimization_barrier((branch, grad_heads))
            branch = lax.psum(branch, "col")
        share_out = Share(grad_low, heads_low, 1)
        grad_query, grad_pairs = attend_back(
            place, edge, query, grad_heads, pairs, outputs, log_total
        )
        if layer == LAYERS - 1:
            branch, grad_pairs = lax.optimization_barrier((branch, grad_pairs))
            output = middle + branch.astype(jnp.float32)
        grad_pairs = beside(grad_pairs, share_down, share_up, share_out, *late)
        grad_pairs = lax.psum_scatter(grad_pairs, "row", scatter_dimension=0, tiled=True)
        grad_pairs = beside(grad_pairs, share_down, share_up)
        grad_mixed = jnp.concatenate(
            [
                grad_query.reshape(row_tokens, slot_count, 2 * HD)[..., :HD],
                grad_pairs.reshape(row_tokens, slot_count, 2 * HD),
            ],
            axis=-1,
        ).reshape(row_tokens, slot_count * 3 * HD)
        incoming = column_sum(contract_cols(grad_mixed, wide_qkv))
        share_qkv = Share(normed_one, grad_mixed)
        if layer:
            incoming = beside(incoming, share_qkv, share_out)
        late = (share_qkv, share_out)
        back_one, gain_part_one, shift_part_one = norm_backward(
            incoming, standard_one, inverse_one, gain_one[layer]
        )
        grad = grad + back_one
        shares[layer] = (share_qkv, share_out, share_up, share_down)
        two = everyone_sum(jnp.stack([gain_part_two, shift_part_two]))
        one = everyone_sum(jnp.stack([gain_part_one, shift_part_one]))
        norm_grads[layer] = (one[0], one[1], two[0], two[1])
    norms = [jnp.stack(parts) for parts in zip(*norm_grads)]
    results = [[share.result() for share in group] for group in shares]
    weights = [
        jnp.stack([part.T if turned else part for part in parts])
        for parts, turned in zip(zip(*results), (False, True, False, True))
    ]
    return (output, grad, *norms, *weights)


def solution(mesh):
    placed = (
        P(("dp", "row"), None),
        P(("dp", "row")),
        P(),
        P(),
        P(),
        P(),
        P(),
        P(None, "row", "col"),
        P(None, "col", "row"),
        P(None, "row", "col"),
        P(None, "col", "row"),
        P(("dp", "row"), None),
    )
    return jax.shard_map(
        body,
        mesh=mesh,
        in_specs=placed,
        out_specs=(
            P(("dp", "row"), None),
            P(("dp", "row"), None),
            P(),
            P(),
            P(),
            P(),
            P(None, "row", "col"),
            P(None, "col", "row"),
            P(None, "row", "col"),
            P(None, "col", "row"),
        ),
        check_vma=False,
    )
```

time: 1390 us -> 1030 us (0.74)
  waiting for transfers between devices: 878 us -> 601 us
  matrix products: 250 us -> 89.7 us
  blocking collectives: 111 us -> 0 us
  starting transfers between devices: 3.31 us -> 66.6 us
  Pallas kernels: 0 us -> 42 us
  local copies, waits for them, and re-layouts: 38.7 us -> 78.7 us
  other arithmetic: 84.7 us -> 122 us
    ppermute x0 -> x54, waiting for transfers between devices: none -> 208 us  [swap(): return lax.ppermute(value, axis, [(i, i ^ bit) for i in range(count)])]
    all_gather x10 -> x2, waiting for transfers between devices: 199 us -> 22.2 us  [body(): lax.all_gather(mixed[..., HD:].reshape(row_tokens, slot_count * 2 * HD),...]
    unnamed x31 -> x12, waiting for transfers between devices: 150 us -> 0.2 us
    dot_general x24 -> x22, matrix products: 195 us -> 46 us  [the longest x16 36.1 us: product(): lax.dot_general(part, right, (((0,), (right_dim,)), ((), ())), preferred_...]
    psum x3 -> x1, waiting for transfers between devices: 161 us -> 28 us  [body(): branch = lax.psum(branch, 'col')]
    reduce_scatter x6 -> x2, waiting for transfers between devices: 133 us -> 6.04 us  [body(): lax.psum_scatter(grad_pairs, 'row', scatter_dimension=0, tiled=True)]
    psum x4 -> x7, waiting for transfers between devices: 235 us -> 337 us  [column_sum(): return lax.psum(pieces.astype(jnp.bfloat16), 'col').astype(jnp.float32)]
    all_gather x9 -> x0, blocking collectives: 86.5 us -> none  [the longest x2 26 us: finish_layer(): lax.all_gather(share_qkv.astype(jnp.bfloat16), 'dp', axis=0, tiled=True)]
  transfers between devices with their start and end apart: 27 -> 66, of which waited for: 24 -> 33; matrix products, arithmetic and copies ran while one was open for 15% -> 18% of each run, Pallas kernels for 0% -> 4%
where the time goes in v1:
time: 1030 us; the launch traced here: 1020 us
  waiting for transfers between devices  601 us (58%)
  other arithmetic  122 us (12%)
  matrix products  89.7 us (9%)
  local copies, waits for them, and re-layouts  78.7 us (8%)
  starting transfers between devices  66.6 us (6%)
  Pallas kernels  42 us (4%)
  between operations  16.5 us (2%)
    psum x7, waiting for transfers between devices, column_sum(): return lax.psum(pieces.astype(jnp.bfloat16), 'col').astype(jnp.float32)  337 us
    ppermute x54, waiting for transfers between devices, swap(): return lax.ppermute(value, axis, [(i, i ^ bit) for i in range(count)])  208 us
    ppermute x54, starting transfers between devices, swap(): return lax.ppermute(value, axis, [(i, i ^ bit) for i in range(count)])  56.2 us
    dot_general x16, matrix products, product(): lax.dot_general(part, right, (((0,), (right_dim,)), ((), ())), preferred_...  36.1 us
    unnamed x315, local copies, waits for them, and re-layouts  33.9 us
    another operation x29, other arithmetic, gather_rows(): jnp.stack([jnp.where(upper, other, held), jnp.where(upper, held, other)],...  31.6 us
    psum x1, waiting for transfers between devices, body(): branch = lax.psum(branch, 'col')  28 us
    pallas_call x2, Pallas kernels, attend_back(): pl.pallas_call(back_kernel, grid=(slots,), in_specs=[scalar, pl.BlockSpec...  25.8 us
  transfers between devices with their start and end apart: 66, of which 33 were waited for; matrix products, arithmetic and copies ran while one was open for 18% of the time, Pallas kernels for 4%

profile of v1, /device:TPU:0, one launch (start us, length us, event | category | flops | bytes accessed | tf_op | source)
XLA Modules:
  0.0 1016.2 jit_solution(14137845774674826218)
XLA Ops:
  12.0 19.4 %collective-permute-done.10 = bf16[272,1536]{1,0:T(8,128)(2,1)} collective-permute-done((bf16[272,1536]{1,0:T(8,128)(2,1)S(1)}, bf16[272,1536]{1,0:T(8,128)(2,1)}, u32[]{:S(2)}, u32[]{:S(2)}) %collective-permute-start.10) | collective-permute-done | bytes 835616 | tf_op jit(solution)/shard_map/ppermute | solution.py:38
  31.4 17.1 %collective-permute-done.2 = bf16[272,1536]{1,0:T(8,128)(2,1)} collective-permute-done((bf16[272,1536]{1,0:T(8,128)(2,1)S(1)}, bf16[272,1536]{1,0:T(8,128)(2,1)}, u32[]{:S(2)}, u32[]{:S(2)}) %collective-permute-start.2) | collective-permute-done | bytes 835616 | tf_op jit(solution)/shard_map/ppermute | solution.py:38
  82.0 18.5 %collective-permute-done.16 = bf16[272,1088]{1,0:T(8,128)(2,1)} collective-permute-done((bf16[272,1088]{1,0:T(8,128)(2,1)}, bf16[272,1088]{1,0:T(8,128)(2,1)}, u32[]{:S(2)}, u32[]{:S(2)}) %collective-permute-start.16) | collective-permute-done | bytes 591904 | tf_op jit(solution)/shard_map/ppermute | solution.py:38
  100.8 26.4 %collective-permute-done.8 = bf16[272,1088]{1,0:T(8,128)(2,1)} collective-permute-done((bf16[272,1088]{1,0:T(8,128)(2,1)S(1)}, bf16[272,1088]{1,0:T(8,128)(2,1)}, u32[]{:S(2)}, u32[]{:S(2)}) %collective-permute-start.8) | collective-permute-done | bytes 591904 | tf_op jit(solution)/shard_map/ppermute | solution.py:38
  127.2 13.4 %collective-permute-done.6 = bf16[272,1088]{1,0:T(8,128)(2,1)} collective-permute-done((bf16[272,1088]{1,0:T(8,128)(2,1)}, bf16[272,1088]{1,0:T(8,128)(2,1)}, u32[]{:S(2)}, u32[]{:S(2)}) %collective-permute-start.6) | collective-permute-done | bytes 591904 | tf_op jit(solution)/shard_map/ppermute | solution.py:38
  140.6 13.4 %collective-permute-done.14 = bf16[272,1088]{1,0:T(8,128)(2,1)} collective-permute-done((bf16[272,1088]{1,0:T(8,128)(2,1)S(1)}, bf16[272,1088]{1,0:T(8,128)(2,1)}, u32[]{:S(2)}, u32[]{:S(2)}) %collective-permute-start.14) | collective-permute-done | bytes 591904 | tf_op jit(solution)/shard_map/ppermute | solution.py:38
  159.9 4.8 collective-permute-done.4
  178.1 8.1 shard_map.195
  197.0 64.5 %all-reduce.13.cloned.1.call-done = bf16[512,1088]{0,1:T(8,128)(2,1)} async-done(((bf16[512,1088]{0,1:T(8,128)(2,1)}), bf16[512,1088]{0,1:T(8,128)(2,1)}) %all-reduce.13.cloned.1.call-update) | async-done | bytes 1114128 | tf_op jit(solution)/shard_map/psum | solution.py:66
  266.7 7.9 multiply_convert_fusion.1
  282.5 49.3 %all-reduce.15.cloned.1.call-done = bf16[512,1088]{0,1:T(8,128)(2,1)} async-done(((bf16[512,1088]{0,1:T(8,128)(2,1)}), bf16[512,1088]{0,1:T(8,128)(2,1)}) %all-reduce.15.cloned.1.call-update) | async-done | bytes 1114128 | tf_op jit(solution)/shard_map/psum | solution.py:66
  355.2 22.2 %all-gather.5.cloned.1.call-done.pairs = bf16[2048,1024]{1,0:T(8,128)(2,1)} async-done(((bf16[512,1024]{1,0:T(8,128)(2,1)}), bf16[2048,1024]{1,0:T(8,128)(2,1)}) %all-gather.5.cloned.1.call-update) | async-done | bytes 4194320 | tf_op jit(solution)/shard_map/all_gather | solution.py:333
  379.6 8.1 shard_map.196
  390.5 8.7 all-reduce.19.cloned.1.call-start
  406.3 55.3 %all-reduce.17.cloned.1.call-done = bf16[512,1088]{0,1:T(8,128)(2,1)} async-done(((bf16[512,1088]{0,1:T(8,128)(2,1)}), bf16[512,1088]{0,1:T(8,128)(2,1)}) %all-reduce.17.cloned.1.call-update) | async-done | bytes 1114128 | tf_op jit(solution)/shard_map/psum | solution.py:66
  466.6 11.5 %multiply_convert_fusion = (bf16[512,1088]{0,1:T(8,128)(2,1)S(1)}, f32[512,1088]{0,1:T(8,128)S(1)}, f32[512,1088]{0,1:T(8,128)S(1)}) fusion(bf16[512,1088]{0,1:T(8,128)(2,1)S(1)} %add_convert_fusion.2, bf16[1088,1088]{1,0:T(8,128)(2,1)S(1)} %bitcast.405), kind=kOutput, calls=%fused_computation.60 | convolution fusion | flops 1248362496 | bytes 9052160 | tf_op jit(solution)/shard_map/dot_general | solution.py:347
  499.0 43.0 %all-reduce.19.cloned.1.call-done = bf16[512,1088]{0,1:T(8,128)(2,1)} async-done(((bf16[512,1088]{0,1:T(8,128)(2,1)}), bf16[512,1088]{0,1:T(8,128)(2,1)}) %all-reduce.19.cloned.1.call-update) | async-done | bytes 1114128 | tf_op jit(solution)/shard_map/psum | solution.py:66
  562.3 12.9 %shard_map.197 = (bf16[512,1024]{1,0:T(8,128)(2,1)S(1)}, bf16[2048,1024]{1,0:T(8,128)(2,1)S(1)}) custom-call(s32[1]{0:T(128)} %bitcast.place, s32[1,512]{1,0:T(1,128)S(1)} %bitcast.349, bf16[512,1024]{1,0:T(8,128)(2,1)S(1)} %copy.72.query, bf16[512,1024]{1,0:T(8,128)(2,1)S(1)} %copy-done.6, bf16[2048,1024]{1,0:T(8,128)(2,1)S(1)} %copy-done.10, ...), custom_call_target="tpu_custom_call" | custom-call | flops 34359738368 | bytes 12582912 | tf_op jit(solution)/shard_map/pallas_call | solution.py:262
  577.3 28.0 %all-reduce.21.cloned.1.call-done = bf16[512,1088]{0,1:T(8,128)(2,1)} async-done(((bf16[512,1088]{0,1:T(8,128)(2,1)}), bf16[512,1088]{0,1:T(8,128)(2,1)}) %all-reduce.21.cloned.1.call-update) | async-done | bytes 1114128 | tf_op jit(solution)/shard_map/psum | solution.py:415
  625.0 20.9 %collective-permute-done.48 = f32[2,1088]{1,0:T(2,128)S(1)} collective-permute-done((f32[2,1088]{1,0:T(2,128)S(1)}, f32[2,1088]{1,0:T(2,128)S(1)}, u32[]{:S(2)}, u32[]{:S(2)}) %collective-permute-start.48) | collective-permute-done | bytes 8736 | tf_op jit(solution)/shard_map/ppermute | solution.py:38
  646.0 6.0 reduce-scatter.3.cloned.1.call-done
  666.4 47.3 %all-reduce.23.cloned.1.call-done = bf16[512,1088]{0,1:T(8,128)(2,1)} async-done(((bf16[512,1088]{0,1:T(8,128)(2,1)}), bf16[512,1088]{0,1:T(8,128)(2,1)}) %all-reduce.23.cloned.1.call-update) | async-done | bytes 1114128 | tf_op jit(solution)/shard_map/psum | solution.py:66
  745.1 34.5 %all-reduce.25.cloned.1.call-done = bf16[512,1088]{0,1:T(8,128)(2,1)} async-done(((bf16[512,1088]{0,1:T(8,128)(2,1)}), bf16[512,1088]{0,1:T(8,128)(2,1)}) %all-reduce.25.cloned.1.call-update) | async-done | bytes 1114128 | tf_op jit(solution)/shard_map/psum | solution.py:66
  799.4 12.9 %shard_map.198 = (bf16[512,1024]{1,0:T(8,128)(2,1)S(1)}, bf16[2048,1024]{1,0:T(8,128)(2,1)S(1)}) custom-call(s32[1]{0:T(128)} %bitcast.place, s32[1,512]{1,0:T(1,128)S(1)} %bitcast.350, bf16[512,1024]{1,0:T(8,128)(2,1)S(1)} %copy-done.5, bf16[512,1024]{1,0:T(8,128)(2,1)S(1)} %copy.77.grads, bf16[2048,1024]{1,0:T(8,128)(2,1)S(1)} %copy-done.8, ...), custom_call_target="tpu_custom_call" | custom-call | flops 34359738368 | bytes 12582912 | tf_op jit(solution)/shard_map/pallas_call | solution.py:262
  824.1 10.0 collective-permute-start.41
  839.6 5.9 collective-permute-start.43
  864.2 11.6 %collective-permute-done.52 = bf16[272,512]{1,0:T(8,128)(2,1)S(1)} collective-permute-done((bf16[272,512]{1,0:T(8,128)(2,1)S(1)}, bf16[272,512]{1,0:T(8,128)(2,1)S(1)}, u32[]{:S(2)}, u32[]{:S(2)}) %collective-permute-start.52) | collective-permute-done | bytes 278560 | tf_op jit(solution)/shard_map/ppermute | solution.py:38
  878.9 15.8 %collective-permute-done.53 = bf16[272,512]{1,0:T(8,128)(2,1)S(1)} collective-permute-done((bf16[272,512]{1,0:T(8,128)(2,1)S(1)}, bf16[272,512]{1,0:T(8,128)(2,1)S(1)}, u32[]{:S(2)}, u32[]{:S(2)}) %collective-permute-start.53) | collective-permute-done | bytes 278560 | tf_op jit(solution)/shard_map/ppermute | solution.py:38
  900.5 5.4 convolution_convert_fusion.6
  915.2 43.2 %all-reduce.27.cloned.1.call-done = bf16[512,1088]{0,1:T(8,128)(2,1)} async-done(((bf16[512,1088]{0,1:T(8,128)(2,1)}), bf16[512,1088]{0,1:T(8,128)(2,1)}) %all-reduce.27.cloned.1.call-update) | async-done | bytes 1114128 | tf_op jit(solution)/shard_map/psum | solution.py:66
  970.9 16.1 %collective-permute-done.50 = bf16[272,1536]{1,0:T(8,128)(2,1)S(1)} collective-permute-done((bf16[272,1536]{1,0:T(8,128)(2,1)S(1)}, bf16[272,1536]{1,0:T(8,128)(2,1)S(1)}, u32[]{:S(2)}, u32[]{:S(2)}) %collective-permute-start.50) | collective-permute-done | bytes 835616 | tf_op jit(solution)/shard_map/ppermute | solution.py:38
  990.1 16.8 %collective-permute-done.51 = bf16[272,1536]{1,0:T(8,128)(2,1)S(1)} collective-permute-done((bf16[272,1536]{1,0:T(8,128)(2,1)S(1)}, bf16[272,1536]{1,0:T(8,128)(2,1)S(1)}, u32[]{:S(2)}, u32[]{:S(2)}) %collective-permute-start.51) | collective-permute-done | bytes 835616 | tf_op jit(solution)/shard_map/ppermute | solution.py:38
  (653 shorter events, 320.7 us)
Async XLA Ops:
  7.2 168.3 %all-gather.3.cloned.1.call-start = ((), (), s32[]{:S(2)}) async-start(), calls=%async_computation.2 | async-start | bytes 5242880 | tf_op jit(solution)/shard_map/all_gather | solution.py:333
  69.9 191.5 %all-reduce.13.cloned.1.call-start = ((), (), s32[]{:S(2)}) async-start(), calls=%async_computation.3 | async-start | bytes 2228224 | tf_op jit(solution)/shard_map/psum | solution.py:66
  74.3 52.9 %collective-permute-start.8 = (bf16[272,1088]{1,0:T(8,128)(2,1)S(1)}, bf16[272,1088]{1,0:T(8,128)(2,1)}, u32[]{:S(2)}, u32[]{:S(2)}) collective-permute-start(bf16[272,1088]{1,0:T(8,128)(2,1)S(1)} %get-tuple-element.165), channel_id=1, source_target_pairs={{0,8},{4,12},{8,0},{12,4},{1,9},{5,13},{9,1},{13,5},{2,10},{6,14},... | collective-permute-start | bytes 1775624 | tf_op jit(solution)/shard_map/ppermute | solution.py:38
  76.9 63.7 %collective-permute-start.6 = (bf16[272,1088]{1,0:T(8,128)(2,1)}, bf16[272,1088]{1,0:T(8,128)(2,1)}, u32[]{:S(2)}, u32[]{:S(2)}) collective-permute-start(bf16[272,1088]{1,0:T(8,128)(2,1)} %get-tuple-element.161), channel_id=1, source_target_pairs={{0,8},{4,12},{8,0},{12,4},{1,9},{5,13},{9,1},{13,5},{2,10},{6,14},... | collective-permute-start | bytes 1775624 | tf_op jit(solution)/shard_map/ppermute | solution.py:38
  77.3 76.8 %collective-permute-start.14 = (bf16[272,1088]{1,0:T(8,128)(2,1)S(1)}, bf16[272,1088]{1,0:T(8,128)(2,1)}, u32[]{:S(2)}, u32[]{:S(2)}) collective-permute-start(bf16[272,1088]{1,0:T(8,128)(2,1)S(1)} %get-tuple-element.160), channel_id=1, source_target_pairs={{0,8},{4,12},{8,0},{12,4},{1,9},{5,13},{9,1},{13,5},{2,10},{6,14},... | collective-permute-start | bytes 1775624 | tf_op jit(solution)/shard_map/ppermute | solution.py:38
  81.0 79.0 %collective-permute-start.12 = (bf16[272,512]{1,0:T(8,128)(2,1)S(1)}, bf16[272,512]{1,0:T(8,128)(2,1)S(1)}, u32[]{:S(2)}, u32[]{:S(2)}) collective-permute-start(bf16[272,512]{1,0:T(8,128)(2,1)S(1)} %get-tuple-element.192), channel_id=1, source_target_pairs={{0,8},{4,12},{8,0},{12,4},{1,9},{5,13},{9,1},{13,5},{2,10},{6,14},... | collective-permute-start | bytes 835592 | tf_op jit(solution)/shard_map/ppermute | solution.py:38
  100.5 64.3 %collective-permute-start.4 = (bf16[272,512]{1,0:T(8,128)(2,1)S(1)}, bf16[272,512]{1,0:T(8,128)(2,1)S(1)}, u32[]{:S(2)}, u32[]{:S(2)}) collective-permute-start(bf16[272,512]{1,0:T(8,128)(2,1)S(1)} %get-tuple-element.193), channel_id=1, source_target_pairs={{0,8},{4,12},{8,0},{12,4},{1,9},{5,13},{9,1},{13,5},{2,10},{6,14},... | collective-permute-start | bytes 835592 | tf_op jit(solution)/shard_map/ppermute | solution.py:38
  168.9 109.5 %collective-permute-start.11 = (bf16[2,272,1536]{2,1,0:T(8,128)(2,1)}, bf16[2,272,1536]{2,1,0:T(8,128)(2,1)}, u32[]{:S(2)}, u32[]{:S(2)}) collective-permute-start(bf16[2,272,1536]{2,1,0:T(8,128)(2,1)} %pad_maximum_fusion.10), channel_id=1, source_target_pairs={{0,4},{4,0},{8,12},{12,8},{1,5},{5,1},{9,13},{13,9},{2,6},{6,2},{1... | collective-permute-start | bytes 5013512 | tf_op jit(solution)/shard_map/ppermute | solution.py:38
  189.7 142.1 %all-reduce.15.cloned.1.call-start = ((), (), s32[]{:S(2)}) async-start(), calls=%async_computation.4 | async-start | bytes 2228224 | tf_op jit(solution)/shard_map/psum | solution.py:66
  278.3 99.1 %all-gather.5.cloned.1.call-start = ((), (), s32[]{:S(2)}) async-start(), calls=%async_computation.5 | async-start | bytes 5242880 | tf_op jit(solution)/shard_map/all_gather | solution.py:333
  343.3 118.4 %all-reduce.17.cloned.1.call-start = ((), (), s32[]{:S(2)}) async-start(), calls=%async_computation.6 | async-start | bytes 2228224 | tf_op jit(solution)/shard_map/psum | solution.py:66
  347.6 55.1 %collective-permute-start.15 = (bf16[2,272,1088]{2,1,0:T(8,128)(2,1)}, bf16[2,272,1088]{2,1,0:T(8,128)(2,1)}, u32[]{:S(2)}, u32[]{:S(2)}) collective-permute-start(bf16[2,272,1088]{2,1,0:T(8,128)(2,1)} %pad_maximum_fusion.16), channel_id=1, source_target_pairs={{0,4},{4,0},{8,12},{12,8},{1,5},{5,1},{9,13},{13,9},{2,6},{6,2},{1... | collective-permute-start | bytes 3551240 | tf_op jit(solution)/shard_map/ppermute | solution.py:38
  390.5 151.5 %all-reduce.19.cloned.1.call-start = ((), (), s32[]{:S(2)}) async-start(), calls=%async_computation.7 | async-start | bytes 2228224 | tf_op jit(solution)/shard_map/psum | solution.py:66
  480.1 63.6 %collective-permute-start.18 = (bf16[544,1088]{1,0:T(8,128)(2,1)}, bf16[544,1088]{1,0:T(8,128)(2,1)}, u32[]{:S(2)}, u32[]{:S(2)}) collective-permute-start(bf16[544,1088]{1,0:T(8,128)(2,1)} %convolution_convert_fusion.5), channel_id=1, source_target_pairs={{0,4},{4,0},{8,12},{12,8},{1,5},{5,1},{9,13},{13,9},{2,6},{6,2},{1... | collective-permute-start | bytes 3551240 | tf_op jit(solution)/shard_map/ppermute | solution.py:38
  485.4 58.3 %collective-permute-start.19 = (bf16[544,1088]{1,0:T(8,128)(2,1)}, bf16[544,1088]{1,0:T(8,128)(2,1)}, u32[]{:S(2)}, u32[]{:S(2)}) collective-permute-start(bf16[544,1088]{1,0:T(8,128)(2,1)} %convolution_convert_fusion.4), channel_id=1, source_target_pairs={{0,4},{4,0},{8,12},{12,8},{1,5},{5,1},{9,13},{13,9},{2,6},{6,2},{1... | collective-permute-start | bytes 3551240 | tf_op jit(solution)/shard_map/ppermute | solution.py:38
  488.5 116.8 %all-reduce.21.cloned.1.call-start = ((), (), s32[]{:S(2)}) async-start(), calls=%async_computation.8 | async-start | bytes 2228224 | tf_op jit(solution)/shard_map/psum | solution.py:415
  551.8 100.2 %reduce-scatter.3.cloned.1.call-start = ((), (), s32[]{:S(2)}) async-start(), calls=%async_computation.9 | async-start | bytes 5242880 | tf_op jit(solution)/shard_map/reduce_scatter | solution.py:424
  555.4 49.9 %collective-permute-start.20 = (bf16[272,1088]{1,0:T(8,128)(2,1)}, bf16[272,1088]{1,0:T(8,128)(2,1)S(1)}, u32[]{:S(2)}, u32[]{:S(2)}) collective-permute-start(bf16[272,1088]{1,0:T(8,128)(2,1)} %fusion.32), channel_id=1, source_target_pairs={{0,8},{4,12},{8,0},{12,4},{1,9},{5,13},{9,1},{13,5},{2,10},{6,14},... | collective-permute-start | bytes 1775624 | tf_op jit(solution)/shard_map/ppermute | solution.py:38
  559.5 45.8 %collective-permute-start.21 = (bf16[272,1088]{1,0:T(8,128)(2,1)}, bf16[272,1088]{1,0:T(8,128)(2,1)}, u32[]{:S(2)}, u32[]{:S(2)}) collective-permute-start(bf16[272,1088]{1,0:T(8,128)(2,1)} %fusion.33), channel_id=1, source_target_pairs={{0,8},{4,12},{8,0},{12,4},{1,9},{5,13},{9,1},{13,5},{2,10},{6,14},... | collective-permute-start | bytes 1775624 | tf_op jit(solution)/shard_map/ppermute | solution.py:38
  562.3 43.0 %collective-permute-start.22 = (bf16[544,512]{1,0:T(8,128)(2,1)}, bf16[544,512]{1,0:T(8,128)(2,1)}, u32[]{:S(2)}, u32[]{:S(2)}) collective-permute-start(bf16[544,512]{1,0:T(8,128)(2,1)} %convolution_convert_fusion.17), channel_id=1, source_target_pairs={{0,4},{4,0},{8,12},{12,8},{1,5},{5,1},{9,13},{13,9},{2,6},{6,2},{1... | collective-permute-start | bytes 1671176 | tf_op jit(solution)/shard_map/ppermute | solution.py:38
  605.3 108.4 %all-reduce.23.cloned.1.call-start = ((), (), s32[]{:S(2)}) async-start(), calls=%async_computation.10 | async-start | bytes 2228224 | tf_op jit(solution)/shard_map/psum | solution.py:66
  655.9 59.3 %collective-permute-start.25 = (bf16[544,1536]{1,0:T(8,128)(2,1)}, bf16[544,1536]{1,0:T(8,128)(2,1)}, u32[]{:S(2)}, u32[]{:S(2)}) collective-permute-start(bf16[544,1536]{1,0:T(8,128)(2,1)} %convolution_convert_fusion.3), channel_id=1, source_target_pairs={{0,4},{4,0},{8,12},{12,8},{1,5},{5,1},{9,13},{13,9},{2,6},{6,2},{1... | collective-permute-start | bytes 5013512 | tf_op jit(solution)/shard_map/ppermute | solution.py:38
  659.7 119.9 %all-reduce.25.cloned.1.call-start = ((), (), s32[]{:S(2)}) async-start(), calls=%async_computation.11 | async-start | bytes 2228224 | tf_op jit(solution)/shard_map/psum | solution.py:66
  661.9 53.4 %collective-permute-start.26 = (bf16[272,512]{1,0:T(8,128)(2,1)}, bf16[272,512]{1,0:T(8,128)(2,1)}, u32[]{:S(2)}, u32[]{:S(2)}) collective-permute-start(bf16[272,512]{1,0:T(8,128)(2,1)} %fusion.38), channel_id=1, source_target_pairs={{0,8},{4,12},{8,0},{12,4},{1,9},{5,13},{9,1},{13,5},{2,10},{6,14},... | collective-permute-start | bytes 835592 | tf_op jit(solution)/shard_map/ppermute | solution.py:38
  726.1 170.6 %reduce-scatter.5.cloned.1.call-start = ((), (), s32[]{:S(2)}) async-start(), calls=%async_computation.12 | async-start | bytes 5242880 | tf_op jit(solution)/shard_map/reduce_scatter | solution.py:424
  729.7 51.5 %collective-permute-start.27 = (bf16[544,1088]{1,0:T(8,128)(2,1)}, bf16[544,1088]{1,0:T(8,128)(2,1)}, u32[]{:S(2)}, u32[]{:S(2)}) collective-permute-start(bf16[544,1088]{1,0:T(8,128)(2,1)} %convolution_convert_fusion.2), channel_id=1, source_target_pairs={{0,4},{4,0},{8,12},{12,8},{1,5},{5,1},{9,13},{13,9},{2,6},{6,2},{1... | collective-permute-start | bytes 3551240 | tf_op jit(solution)/shard_map/ppermute | solution.py:38
  731.7 49.5 %collective-permute-start.28 = (bf16[544,1088]{1,0:T(8,128)(2,1)}, bf16[544,1088]{1,0:T(8,128)(2,1)}, u32[]{:S(2)}, u32[]{:S(2)}) collective-permute-start(bf16[544,1088]{1,0:T(8,128)(2,1)} %convolution_convert_fusion.1), channel_id=1, source_target_pairs={{0,4},{4,0},{8,12},{12,8},{1,5},{5,1},{9,13},{13,9},{2,6},{6,2},{1... | collective-permute-start | bytes 3551240 | tf_op jit(solution)/shard_map/ppermute | solution.py:38
  735.5 45.7 %collective-permute-start.29 = (bf16[272,1536]{1,0:T(8,128)(2,1)}, bf16[272,1536]{1,0:T(8,128)(2,1)}, u32[]{:S(2)}, u32[]{:S(2)}) collective-permute-start(bf16[272,1536]{1,0:T(8,128)(2,1)} %fusion.30), channel_id=1, source_target_pairs={{0,8},{4,12},{8,0},{12,4},{1,9},{5,13},{9,1},{13,5},{2,10},{6,14},... | collective-permute-start | bytes 2506760 | tf_op jit(solution)/shard_map/ppermute | solution.py:38
  738.7 42.4 %collective-permute-start.30 = (bf16[272,512]{1,0:T(8,128)(2,1)}, bf16[272,512]{1,0:T(8,128)(2,1)S(1)}, u32[]{:S(2)}, u32[]{:S(2)}) collective-permute-start(bf16[272,512]{1,0:T(8,128)(2,1)} %fusion.37), channel_id=1, source_target_pairs={{0,16},{16,0},{1,17},{17,1},{2,18},{18,2},{3,19},{19,3},{4,20},{20... | collective-permute-start | bytes 835592 | tf_op jit(solution)/shard_map/ppermute | solution.py:38
  740.2 83.8 %collective-permute-start.40 = (f32[2,1088]{1,0:T(2,128)S(1)}, f32[2,1088]{1,0:T(2,128)S(1)}, u32[]{:S(2)}, u32[]{:S(2)}) collective-permute-start(f32[2,1088]{1,0:T(2,128)S(1)} %pad_maximum_fusion.23), channel_id=1, source_target_pairs={{0,4},{4,0},{8,12},{12,8},{1,5},{5,1},{9,13},{13,9},{2,6},{6,2},{1... | collective-permute-start | bytes 26120 | tf_op jit(solution)/shard_map/ppermute | solution.py:38
  820.4 138.0 %all-reduce.27.cloned.1.call-start = ((), (), s32[]{:S(2)}) async-start(), calls=%async_computation.13 | async-start | bytes 2228224 | tf_op jit(solution)/shard_map/psum | solution.py:66
  909.3 54.3 %collective-permute-start.49 = (bf16[544,1536]{1,0:T(8,128)(2,1)}, bf16[544,1536]{1,0:T(8,128)(2,1)}, u32[]{:S(2)}, u32[]{:S(2)}) collective-permute-start(bf16[544,1536]{1,0:T(8,128)(2,1)} %convolution_convert_fusion), channel_id=1, source_target_pairs={{0,4},{4,0},{8,12},{12,8},{1,5},{5,1},{9,13},{13,9},{2,6},{6,2},{1... | collective-permute-start | bytes 5013512 | tf_op jit(solution)/shard_map/ppermute | solution.py:38
  (191 other events, 2282.6 us)
Sparse Core Ops, SparseCore 0:
  70.0 58.5 all-gather.2
  189.8 71.6 all-reduce.12
  278.4 53.3 all-reduce.14
  343.4 33.9 all-gather.4
  390.6 71.0 all-reduce.16
  488.6 53.3 all-reduce.18
  551.9 53.2 all-reduce.20
  608.0 43.9 reduce-scatter.2
  659.8 53.8 all-reduce.22
  726.2 53.3 all-reduce.24
  820.5 64.3 reduce-scatter.4
  906.0 52.2 all-reduce.26
